TPU v7x, 256 devices: a whole 4x4x8 slice. The times are simulated.
256 devices in a mesh: seg: 8 (over y, core), coil: 16 (over x, z_lo), tile: 2 (over z_hi).
Axes of the slice: x: 4, y: 4, z: 8 (z_hi: 2, z_lo: 4; z = z_hi * 4 + z_lo), core: 2. Of those that a mesh axis runs over, the one named last changes fastest.
Arguments:
- right_side: float32 [1024, 128], P(('seg', 'coil', 'tile')), may hold values from -6 to 6
- sensitivity: float32 [32, 1024, 128], P('coil'), may hold values from -0.75 to 0.75
- field_map: float32 [1024, 64], replicated, may hold values from -12 to 12
- seg_map: int32 [1024, 4], replicated, may hold values from 0 to 23, all different within a row; in each aligned block of 1024 rows (0 to 1023, 1024 to 2047, ...) at most 256 rows name the same one
- sample_rows: int32 [24, 2048], P('seg', 'tile'), may hold values from 0 to 1023
- density: float32 [24, 2048, 64], P('seg', 'tile'), may hold values from 0.25 to 4
- step_alpha: float32 [2], replicated, may hold values from 0.15 to 0.35
- step_beta: float32 [2], replicated, may hold values from 0.1 to 0.5
Outputs:
- solution_field: float32 [1024, 128], P(('seg', 'coil', 'tile'))
- residual: float32 [1024, 128], P(('seg', 'coil', 'tile'))
Inputs may be any that keep to these rules, and one draw needn't show every extreme that they name: `seg_map`: each row names 4 different segments; each segment is named by at most 256 tiles, a bound that some block reaches.
All inputs are finite; a program needn't handle non-finite values.
Results may differ from a plain program's by a relative error of at most 0.0001.
Values sent between devices are 32-bit elements; how exact they have to be, the bound alone decides.
No kernel may reach another device: no remote copies, remote signals or barrier semaphores. Data moves between devices by JAX's collectives and lax.ppermute only.
A program may use at most 128 MiB of HBM per device.

v0:
```python
import math
import jax
import jax.numpy as jnp
from jax import lax
from jax.sharding import PartitionSpec as P

SEGS = 24
TV = 64
ITERS = 2
CAP = 256
ridge_weight = 0.25
highest = lax.Precision.HIGHEST


def tile_list(seg_map, segment, slots):
    tile_count = seg_map.shape[0]
    is_member = jnp.any(seg_map == segment, axis=1).astype(jnp.int32)
    live_count = jnp.sum(is_member)
    sort_keys = (1 - is_member) * tile_count + jnp.arange(tile_count, dtype=jnp.int32)
    sorted_tiles = jnp.argsort(sort_keys)
    listed = sorted_tiles[:slots]
    valid_slots = (jnp.arange(slots, dtype=jnp.int32) < live_count).astype(jnp.float32)
    return (listed, valid_slots)


def row_tables(rows_here, listed, valid_slots, tile_count):
    product = rows_here[:, None] * listed[None, :] % tile_count
    angles = product.astype(jnp.float32) * jnp.float32(2.0 * math.pi / tile_count)
    slot_scale = valid_slots[None, :] / jnp.float32(math.sqrt(tile_count))
    return (jnp.cos(angles) * slot_scale, -jnp.sin(angles) * slot_scale)


def column_tables(voxels):
    steps_here = jnp.arange(voxels, dtype=jnp.int32)
    product = steps_here[:, None] * steps_here[None, :] % voxels
    angles = product.astype(jnp.float32) * jnp.float32(2.0 * math.pi / voxels)
    norm_factor = jnp.float32(1.0 / math.sqrt(voxels))
    return (jnp.cos(angles) * norm_factor, -jnp.sin(angles) * norm_factor)


def segment_normal(
    dir_rows, sens_rows, field_rows, seg_time, row_cos, row_sin, col_cos, col_sin, weights
):
    voxels = field_rows.shape[1]
    phase_angle = field_rows * seg_time
    phase_real = jnp.cos(phase_angle)
    phase_imag = -jnp.sin(phase_angle)
    dir_real = dir_rows[:, :voxels]
    dir_imag = dir_rows[:, voxels:]
    image_real = phase_real * dir_real - phase_imag * dir_imag
    image_imag = phase_real * dir_imag + phase_imag * dir_real
    sens_real = sens_rows[..., :voxels]
    sens_imag = sens_rows[..., voxels:]
    coil_real = sens_real * image_real - sens_imag * image_imag
    coil_imag = sens_real * image_imag + sens_imag * image_real
    grid_real = jnp.einsum("mn,cnv->cmv", row_cos, coil_real, precision=highest) - jnp.einsum(
        "mn,cnv->cmv", row_sin, coil_imag, precision=highest
    )
    grid_imag = jnp.einsum("mn,cnv->cmv", row_cos, coil_imag, precision=highest) + jnp.einsum(
        "mn,cnv->cmv", row_sin, coil_real, precision=highest
    )
    kspace_real = jnp.einsum("cmv,vj->cmj", grid_real, col_cos, precision=highest) - jnp.einsum(
        "cmv,vj->cmj", grid_imag, col_sin, precision=highest
    )
    kspace_imag = jnp.einsum("cmv,vj->cmj", grid_real, col_sin, precision=highest) + jnp.einsum(
        "cmv,vj->cmj", grid_imag, col_cos, precision=highest
    )
    kspace_real = kspace_real * weights[None]
    kspace_imag = kspace_imag * weights[None]
    back_real = jnp.einsum("cmj,jv->cmv", kspace_real, col_cos, precision=highest) + jnp.einsum(
        "cmj,jv->cmv", kspace_imag, col_sin, precision=highest
    )
    back_imag = jnp.einsum("cmj,jv->cmv", kspace_imag, col_cos, precision=highest) - jnp.einsum(
        "cmj,jv->cmv", kspace_real, col_sin, precision=highest
    )
    rows_real = jnp.einsum("mn,cmv->cnv", row_cos, back_real, precision=highest) + jnp.einsum(
        "mn,cmv->cnv", row_sin, back_imag, precision=highest
    )
    rows_imag = jnp.einsum("mn,cmv->cnv", row_cos, back_imag, precision=highest) - jnp.einsum(
        "mn,cmv->cnv", row_sin, back_real, precision=highest
    )
    summed_real = jnp.sum(sens_real * rows_real + sens_imag * rows_imag, axis=0)
    summed_imag = jnp.sum(sens_real * rows_imag - sens_imag * rows_real, axis=0)
    result_real = phase_real * summed_real + phase_imag * summed_imag
    result_imag = phase_real * summed_imag - phase_imag * summed_real
    return jnp.concatenate([result_real, result_imag], axis=1)


def gather_direction(own_tiles):
    return lax.all_gather(own_tiles, ("seg", "coil", "tile"), axis=0, tiled=True)


def shards(
    right_side, sensitivity, field_map, seg_map, sample_rows, density, step_alpha, step_beta
):
    seg_local = sample_rows.shape[0]
    tile_count = field_map.shape[0]
    first_segment = lax.axis_index("seg") * seg_local
    col_cos, col_sin = column_tables(TV)
    prepared = []
    for local_seg in range(seg_local):
        segment = first_segment + local_seg
        listed, valid_slots = tile_list(seg_map, segment, CAP)
        row_cos, row_sin = row_tables(sample_rows[local_seg], listed, valid_slots, tile_count)
        seg_time = (segment.astype(jnp.float32) + 0.5) / jnp.float32(SEGS)
        prepared.append(
            (
                listed,
                row_cos,
                row_sin,
                seg_time,
                sensitivity[:, listed],
                field_map[listed],
                density[local_seg],
            )
        )
    direction = right_side
    solution_field = jnp.zeros_like(right_side)
    residual = right_side
    for step in range(ITERS):
        gathered = gather_direction(direction)
        partial_value = jnp.zeros(gathered.shape, jnp.float32)
        for (
            local_listed,
            local_row_cos,
            local_row_sin,
            local_seg_time,
            sens_rows,
            field_rows,
            weights,
        ) in prepared:
            contrib = segment_normal(
                gathered[local_listed],
                sens_rows,
                field_rows,
                local_seg_time,
                local_row_cos,
                local_row_sin,
                col_cos,
                col_sin,
                weights,
            )
            partial_value = partial_value.at[local_listed].add(contrib)
        image = (
            lax.psum_scatter(
                partial_value, ("seg", "coil", "tile"), scatter_dimension=0, tiled=True
            )
            + ridge_weight * direction
        )
        solution_field = solution_field + step_alpha[step] * direction
        residual = residual - step_alpha[step] * image
        direction = residual + step_beta[step] * direction
    return (solution_field, residual)


def solution(mesh):
    placed = (
        P(("seg", "coil", "tile"), None),
        P("coil", None, None),
        P(),
        P(),
        P("seg", "tile"),
        P("seg", "tile", None),
        P(),
        P(),
    )
    return jax.shard_map(
        shards,
        mesh=mesh,
        in_specs=placed,
        out_specs=(P(("seg", "coil", "tile"), None), P(("seg", "coil", "tile"), None)),
        check_vma=False,
    )
```

profile of v0, /device:TPU:2, one launch (start us, length us, event | category | flops | bytes accessed | tf_op | source)
XLA Modules:
  0.0 2122.0 jit_solution(18167346693493669759)
XLA Ops:
  16.2 626.4 %all-gather = f32[256,4,128]{2,1,0:T(4,128)S(1)} all-gather(f32[1,4,128]{2,1,0:T(4,128)S(1)} %bitcast.389), channel_id=1, replica_groups=mesh['seg'=8,'coil'=16,'tile'=2] {'seg','coil','tile'}, dimensions={0}, use_global_device_ids=true | all-gather | bytes 526336 | tf_op jit(solution)/shard_map/all_gather | solution.py:90
  651.2 6.3 fusion.65
  657.6 4.9 fusion.4
  679.7 6.5 fusion.89
  691.1 4.9 fusion.2
  710.9 6.1 fusion.113
  722.0 4.9 fusion
  730.1 5.3 fusion.5
  760.0 4.9 fusion.3
  789.9 6.7 fusion.1
  806.0 4.9 fusion.109
  829.0 247.1 %all-reduce.5.cloned.1.call-done = f32[1024,128]{1,0:T(8,128)} async-done(((f32[1024,128]{1,0:T(8,128)}), f32[1024,128]{1,0:T(8,128)}) %all-reduce.5.cloned.1.call-update) | async-done | bytes 524304
  1078.1 621.9 %all-gather.1 = f32[256,4,128]{2,1,0:T(4,128)S(1)} all-gather(f32[1,4,128]{2,1,0:T(4,128)S(1)} %fusion.641), channel_id=1, replica_groups=mesh['seg'=8,'coil'=16,'tile'=2] {'seg','coil','tile'}, dimensions={0}, use_global_device_ids=true | all-gather | bytes 526336 | tf_op jit(solution)/shard_map/all_gather | solution.py:90
  1701.9 6.4 fusion.57
  1713.2 4.9 fusion.10
  1723.1 6.2 fusion.81
  1734.2 4.9 fusion.8
  1744.2 6.2 fusion.105
  1755.3 4.9 fusion.6
  1762.1 5.3 fusion.11
  1786.1 5.6 subtract_reduce_fusion
  1792.9 6.5 fusion.9
  1824.0 6.9 fusion.7
  1861.3 250.4 %all-reduce.7.cloned.1.call-done = f32[1024,128]{1,0:T(8,128)} async-done(((f32[1024,128]{1,0:T(8,128)}), f32[1024,128]{1,0:T(8,128)}) %all-reduce.7.cloned.1.call-update) | async-done | bytes 524304
  (350 shorter events, 246.4 us)
Async XLA Ops:
  7.2 636.5 %copy-start = (f32[2,1024,128]{2,1,0:T(8,128)S(1)}, f32[2,1024,128]{2,1,0:T(8,128)}, u32[]{:S(2)}) copy-start(f32[2,1024,128]{2,1,0:T(8,128)} %param.9) | copy-start | bytes 3145732
  7.2 1068.9 %all-reduce.5.cloned.1.call-start = ((), (), s32[]{:S(2)}) async-start(), calls=%async_computation | async-start | bytes 1048576
  13.7 643.9 %copy-start.67 = (s32[256]{0:T(256)}, s32[256]{0:T(256)S(1)}, u32[]{:S(2)}) copy-start(s32[256]{0:T(256)S(1)} %get-tuple-element.67) | copy-start | bytes 3076
  644.8 12.8 copy-start.17
  645.5 12.1 copy-start.77
  646.1 11.5 copy-start.60
  646.4 11.3 copy-start.25
  646.4 11.3 copy-start.27
  677.8 13.3 copy-start.81
  679.0 12.1 copy-start.29
  679.0 12.1 copy-start.31
  709.2 12.8 copy-start.21
  709.9 12.0 copy-start.84
  710.2 11.8 copy-start.37
  710.2 11.8 copy-start.39
  789.9 6.8 copy-start.6
  827.6 1284.1 %all-reduce.7.cloned.1.call-start = ((), (), s32[]{:S(2)}) async-start(), calls=%async_computation.1 | async-start | bytes 1048576
  1701.3 11.9 copy-start.45
  1701.3 11.9 copy-start.47
  1723.1 11.1 copy-start.41
  1723.1 11.1 copy-start.43
  1743.8 11.5 copy-start.33
  1743.8 11.5 copy-start.35
  1792.9 6.5 copy-start.8
  (68 other events, 95.1 us)
Sparse Core Ops, SparseCore 0:
  827.7 248.2 all-reduce.4
  1861.4 250.2 all-reduce.6
where the time goes:
time: 2130 us; the launch traced here: 2120 us
  blocking collectives  1250 us (59%)
  waiting for transfers between devices  498 us (23%)
  matrix products  287 us (13%)
  other arithmetic  40 us (2%)
  local copies, waits for them, and re-layouts  32.9 us (2%)
    all_gather x2, blocking collectives, gather_direction(): lax.all_gather(own_tiles, ('seg', 'coil', 'tile'), axis=0, tiled=True)  1250 us
    unnamed x4, waiting for transfers between devices  498 us
  transfers between devices with their start and end apart: 2, of which 2 were waited for; matrix products, arithmetic and copies ran while one was open for 0% of the time, Pallas kernels for 0%

commit v1 on v0

--- a/solution.py
+++ b/solution.py
@@ -3,6 +3,7 @@
 import jax.numpy as jnp
 from jax import lax
 from jax.sharding import PartitionSpec as P
+from jax.lax import all_to_all, axis_size
 
 SEGS = 24
 TV = 64
@@ -10,6 +11,17 @@
 CAP = 256
 ridge_weight = 0.25
 highest = lax.Precision.HIGHEST
+
+
+def fill_streams(m):
+    parts_out = all_to_all(
+        jnp.stack([m for _ in range(axis_size(("seg", "coil", "tile")))], axis=0),
+        ("seg", "coil", "tile"),
+        0,
+        0,
+    )
+    shaped = jnp.concatenate(parts_out, 0)
+    return shaped
 
 
 def tile_list(seg_map, segment, slots):
@@ -87,7 +99,7 @@
 
 
 def gather_direction(own_tiles):
-    return lax.all_gather(own_tiles, ("seg", "coil", "tile"), axis=0, tiled=True)
+    return fill_streams(own_tiles)
 
 
 def shards(

time: 2130 us -> 931 us (0.44)
  blocking collectives: 1250 us -> 30.2 us
    all_gather x2 -> x0, blocking collectives: 1250 us -> none  [gather_direction(): lax.all_gather(own_tiles, ('seg', 'coil', 'tile'), axis=0, tiled=True)]
    all_to_all x0 -> x1, blocking collectives: none -> 30.2 us  [fill_streams(): all_to_all(jnp.stack([m for _ in range(axis_size(('seg', 'coil', 'tile'))...]
  transfers between devices with their start and end apart: 2 -> 3, of which waited for: 2 -> 2; matrix products, arithmetic and copies ran while one was open for 0% -> 3% of each run, Pallas kernels for 0% -> 0%
where the time goes in v1:
time: 931 us; the launch traced here: 922 us
  waiting for transfers between devices  500 us (54%)
  matrix products  289 us (31%)
  other arithmetic  41.2 us (4%)
  local copies, waits for them, and re-layouts  30.8 us (3%)
  blocking collectives  30.2 us (3%)
  between operations  16.5 us (2%)
  starting transfers between devices  14.8 us (2%)
    unnamed x4, waiting for transfers between devices  500 us
    dot_general x6, matrix products, segment_normal(): jnp.einsum('mn,cnv->cmv', row_cos, coil_imag, precision=highest)  38 us
    dot_general x6, matrix products, segment_normal(): jnp.einsum('mn,cnv->cmv', row_sin, coil_real, precision=highest)  37.1 us
    all_to_all x1, blocking collectives, fill_streams(): all_to_all(jnp.stack([m for _ in range(axis_size(('seg', 'coil', 'tile'))...  30.2 us
    dot_general x6, matrix products, segment_normal(): jnp.einsum('mn,cnv->cmv', row_sin, coil_imag, precision=highest)  29.6 us
    dot_general x6, matrix products, segment_normal(): jnp.einsum('mn,cmv->cnv', row_sin, back_imag, precision=highest)  29.4 us
    dot_general x6, matrix products, segment_normal(): jnp.einsum('mn,cnv->cmv', row_cos, coil_real, precision=highest)  29.2 us
    dot_general x6, matrix products, segment_normal(): jnp.einsum('mn,cmv->cnv', row_cos, back_imag, precision=highest)  28.2 us
  transfers between devices with their start and end apart: 3, of which 2 were waited for; matrix products, arithmetic and copies ran while one was open for 3% of the time, Pallas kernels for 0%

profile of v1, /device:TPU:2, one launch (start us, length us, event | category | flops | bytes accessed | tf_op | source)
XLA Modules:
  0.0 922.3 jit_solution(7805666540122124228)
XLA Ops:
  8.8 14.7 %all-to-all-start = ((f32[256,4,128]{2,1,0:T(4,128)}), f32[256,4,128]{2,1,0:T(4,128)S(1)}, u32[]{:S(2)}, u32[]{:S(2)}) async-start(f32[256,4,128]{2,1,0:T(4,128)} %stack.4), calls=%async_computation | async-start | bytes 1048576 | tf_op jit(solution)/shard_map/all_to_all | solution.py:17
  60.4 6.4 fusion.65
  66.8 4.9 fusion.4
  76.8 6.6 fusion.89
  88.3 4.9 fusion.2
  98.6 6.2 fusion.113
  109.6 4.9 fusion
  116.5 5.3 fusion.5
  140.6 5.6 subtract_reduce_fusion.3
  146.6 6.5 fusion.3
  177.7 7.0 fusion.1
  216.5 252.9 %all-reduce.5.cloned.1.call-done = f32[1024,128]{1,0:T(8,128)} async-done(((f32[1024,128]{1,0:T(8,128)}), f32[1024,128]{1,0:T(8,128)}) %all-reduce.5.cloned.1.call-update) | async-done | bytes 524304
  472.6 30.2 %all_to_all.10 = f32[256,4,128]{2,1,0:T(4,128)S(1)} all-to-all(f32[256,4,128]{2,1,0:T(4,128)S(1)} %stack.5), channel_id=1, replica_groups=mesh['seg'=8,'coil'=16,'tile'=2] {'seg','coil','tile'}, dimensions={0} | all-to-all | bytes 1048576 | tf_op jit(solution)/shard_map/all_to_all | solution.py:17
  505.8 6.5 fusion.57
  517.2 4.9 fusion.10
  527.7 6.2 fusion.81
  549.4 6.1 fusion.105
  567.4 5.1 fusion.11
  576.6 4.9 fusion.55
  591.4 5.4 subtract_reduce_fusion
  597.2 6.5 fusion.9
  613.2 4.9 fusion.77
  628.5 6.6 fusion.7
  665.7 246.8 %all-reduce.7.cloned.1.call-done = f32[1024,128]{1,0:T(8,128)} async-done(((f32[1024,128]{1,0:T(8,128)}), f32[1024,128]{1,0:T(8,128)}) %all-reduce.7.cloned.1.call-update) | async-done | bytes 524304
  (351 shorter events, 245.4 us)
Async XLA Ops:
  7.2 23.7 %copy-start = (f32[2,1024,128]{2,1,0:T(8,128)S(1)}, f32[2,1024,128]{2,1,0:T(8,128)}, u32[]{:S(2)}) copy-start(f32[2,1024,128]{2,1,0:T(8,128)} %param.9) | copy-start | bytes 3145732
  8.8 21.1 %copy-start.15 = (f32[1024,64]{0,1:T(8,128)S(1)}, f32[1024,64]{0,1:T(8,128)}, u32[]{:S(2)}) copy-start(f32[1024,64]{0,1:T(8,128)} %param.10) | copy-start | bytes 786436
  8.8 44.5 %all-to-all-start = ((f32[256,4,128]{2,1,0:T(4,128)}), f32[256,4,128]{2,1,0:T(4,128)S(1)}, u32[]{:S(2)}, u32[]{:S(2)}) async-start(f32[256,4,128]{2,1,0:T(4,128)} %stack.4), calls=%async_computation | async-start | bytes 1048576 | tf_op jit(solution)/shard_map/all_to_all | solution.py:17
  23.5 445.8 %all-reduce.5.cloned.1.call-start = ((), (), s32[]{:S(2)}) async-start(), calls=%async_computation.2 | async-start | bytes 1048576
  36.8 38.0 %copy-start.47 = (s32[1024]{0:T(1024)}, s32[1024]{0:T(1024)S(1)}, u32[]{:S(2)}) copy-start(s32[1024]{0:T(1024)S(1)} %pad_clamp_fusion.1) | copy-start | bytes 12292
  44.7 51.7 %copy-start.46 = (s32[1024]{0:T(1024)}, s32[1024]{0:T(1024)S(1)}, u32[]{:S(2)}) copy-start(s32[1024]{0:T(1024)S(1)} %pad_clamp_fusion.2) | copy-start | bytes 12292
  46.5 7.9 copy-start.11
  47.6 124.3 %copy-start.18 = (f32[256,2,128]{0,2,1:T(8,128)}, f32[256,2,128]{0,2,1:T(8,128)S(1)}, u32[]{:S(2)}) copy-start(f32[256,2,128]{0,2,1:T(8,128)S(1)} %copy.93) | copy-start | bytes 786436
  47.8 61.8 %copy-start.16 = (f32[256,2,128]{0,2,1:T(8,128)}, f32[256,2,128]{0,2,1:T(8,128)S(1)}, u32[]{:S(2)}) copy-start(f32[256,2,128]{0,2,1:T(8,128)S(1)} %copy.87) | copy-start | bytes 786436
  54.7 12.0 %copy-start.36 = (f32[256,64]{0,1:T(8,128)}, f32[256,64]{0,1:T(8,128)S(1)}, u32[]{:S(2)}) copy-start(f32[256,64]{0,1:T(8,128)S(1)} %get-tuple-element.42) | copy-start | bytes 196612
  54.7 12.0 %copy-start.38 = (f32[256,64]{0,1:T(8,128)}, f32[256,64]{0,1:T(8,128)S(1)}, u32[]{:S(2)}) copy-start(f32[256,64]{0,1:T(8,128)S(1)} %get-tuple-element.43) | copy-start | bytes 196612
  76.1 12.2 %copy-start.34 = (f32[256,64]{0,1:T(8,128)}, f32[256,64]{0,1:T(8,128)S(1)}, u32[]{:S(2)}) copy-start(f32[256,64]{0,1:T(8,128)S(1)} %get-tuple-element.46) | copy-start | bytes 196612
  76.1 12.2 %copy-start.35 = (f32[256,64]{0,1:T(8,128)}, f32[256,64]{0,1:T(8,128)S(1)}, u32[]{:S(2)}) copy-start(f32[256,64]{0,1:T(8,128)S(1)} %get-tuple-element.47) | copy-start | bytes 196612
  97.8 11.8 %copy-start.28 = (f32[256,64]{0,1:T(8,128)}, f32[256,64]{0,1:T(8,128)S(1)}, u32[]{:S(2)}) copy-start(f32[256,64]{0,1:T(8,128)S(1)} %get-tuple-element.50) | copy-start | bytes 196612
  97.8 11.8 %copy-start.30 = (f32[256,64]{0,1:T(8,128)}, f32[256,64]{0,1:T(8,128)S(1)}, u32[]{:S(2)}) copy-start(f32[256,64]{0,1:T(8,128)S(1)} %get-tuple-element.51) | copy-start | bytes 196612
  146.6 6.6 copy-start.6
  215.2 697.3 %all-reduce.7.cloned.1.call-start = ((), (), s32[]{:S(2)}) async-start(), calls=%async_computation.3 | async-start | bytes 1048576
  505.1 12.1 %copy-start.40 = (f32[256,64]{0,1:T(8,128)}, f32[256,64]{0,1:T(8,128)S(1)}, u32[]{:S(2)}) copy-start(f32[256,64]{0,1:T(8,128)S(1)} %get-tuple-element.30) | copy-start | bytes 196612
  505.1 12.1 %copy-start.42 = (f32[256,64]{0,1:T(8,128)}, f32[256,64]{0,1:T(8,128)S(1)}, u32[]{:S(2)}) copy-start(f32[256,64]{0,1:T(8,128)S(1)} %get-tuple-element.31) | copy-start | bytes 196612
  527.0 11.8 %copy-start.32 = (f32[256,64]{0,1:T(8,128)}, f32[256,64]{0,1:T(8,128)S(1)}, u32[]{:S(2)}) copy-start(f32[256,64]{0,1:T(8,128)S(1)} %get-tuple-element.34) | copy-start | bytes 196612
  527.0 11.8 %copy-start.33 = (f32[256,64]{0,1:T(8,128)}, f32[256,64]{0,1:T(8,128)S(1)}, u32[]{:S(2)}) copy-start(f32[256,64]{0,1:T(8,128)S(1)} %get-tuple-element.35) | copy-start | bytes 196612
  548.7 11.8 %copy-start.24 = (f32[256,64]{0,1:T(8,128)}, f32[256,64]{0,1:T(8,128)S(1)}, u32[]{:S(2)}) copy-start(f32[256,64]{0,1:T(8,128)S(1)} %get-tuple-element.38) | copy-start | bytes 196612
  548.7 11.8 %copy-start.26 = (f32[256,64]{0,1:T(8,128)}, f32[256,64]{0,1:T(8,128)S(1)}, u32[]{:S(2)}) copy-start(f32[256,64]{0,1:T(8,128)S(1)} %get-tuple-element.39) | copy-start | bytes 196612
  597.2 6.5 copy-start.4
  (68 other events, 85.7 us)
Sparse Core Ops, SparseCore 0:
  215.3 253.9 all-reduce.4
  665.8 246.6 all-reduce.6
